TPU v7x, 128 devices: a whole 4x4x4 slice. The times are simulated.
128 devices in a mesh: row: 16 (over x, y), col: 8 (over z, core).
Axes of the slice: x: 4, y: 4, z: 4, core: 2. Of those that a mesh axis runs over, the one named last changes fastest.
Arguments:
- amp_store: bfloat16 [32768, 1024], P(('row', 'col')), may hold values from -6 to 6
- store_map: int32 [32768], P(('row', 'col')), may hold values from 0 to 32767, as said below
- integrals: bfloat16 [32768, 32768], P('row', 'col'), may hold values from -0.09375 to 0.09375
- occ_irrep: int32 [100], replicated, may hold values from 0 to 7
- virt_irrep: int32 [800], replicated, may hold values from 0 to 7
- occ_orbs: int32 [2, 1024], replicated, may hold values from 0 to 99
- k_orbs: int32 [2, 32768], P(None, 'col'), may hold values from 0 to 799
- m_orbs: int32 [2, 32768], P(None, 'row'), may hold values from 0 to 799
Outputs:
- ladder: bfloat16 [32768, 1024], P('row', 'col')
Inputs may be any that keep to these rules, and one draw needn't show every extreme that they name: store_map is a permutation. Grid position k belongs to the block of device (r, c) with c = k // 4096 and r = (k % 4096) // 256; the stored rows of device s = r' * 8 + c' (its shard of amp_store) send exactly 2 rows to every device's block, and within block (r, c) those rows fill positions s * 2 to s * 2 + 1.
All inputs are finite; a program needn't handle non-finite values.
Results may differ from a plain program's by a relative error of at most 0.001.
Values may be sent and summed in bfloat16 or wider, within the bound.
No kernel may reach another device: no remote copies, remote signals or barrier semaphores. Data moves between devices by JAX's collectives and lax.ppermute only.
A program may use at most 192 MiB of HBM per device.

v0:
```python
import jax
import jax.numpy as jnp
from jax import lax
from jax.sharding import PartitionSpec as P


def pair_irrep(labels, orbitals):
    return jnp.bitwise_xor(labels[orbitals[0]], labels[orbitals[1]])


def redistribute(buffer):
    return lax.all_to_all(buffer, ("row", "col"), split_axis=0, concat_axis=0, tiled=True)


def body(amp_store, store_map, integrals, occ_irrep, virt_irrep, occ_orbs, k_orbs, m_orbs):
    row_count = lax.axis_size("row")
    col_count = lax.axis_size("col")
    dev_count = row_count * col_count
    stored = amp_store.shape[0]
    slot_count = stored // dev_count
    kblock = k_orbs.shape[1]
    my_row = lax.axis_index("row")
    my_col = lax.axis_index("col")
    myself = my_row * col_count + my_col
    occ_sym = pair_irrep(occ_irrep, occ_orbs)
    k_sym = pair_irrep(virt_irrep, k_orbs)
    m_sym = pair_irrep(virt_irrep, m_orbs)
    naught = jnp.zeros((), amp_store.dtype)
    owner_col = store_map // kblock
    owner_row = store_map % kblock // stored
    within = store_map % stored - myself * slot_count
    place = (owner_row * col_count + owner_col) * slot_count + within
    ordered = jnp.zeros_like(amp_store).at[place].set(amp_store)
    grid_rows = redistribute(ordered)
    own_sym = lax.dynamic_slice_in_dim(k_sym, my_row * stored, stored)
    masked = jnp.where(own_sym[:, None] == occ_sym[None, :], grid_rows, naught)
    screened = jnp.where(m_sym[:, None] == k_sym[None, :], integrals, naught)
    partial_sum = jnp.dot(
        screened,
        lax.all_gather(masked, "row", axis=0, tiled=True),
        preferred_element_type=jnp.float32,
    )
    return lax.psum_scatter(partial_sum, "col", scatter_dimension=1, tiled=True).astype(
        jnp.bfloat16
    )


def solution(mesh):
    in_specs = (
        P(("row", "col"), None),
        P(("row", "col")),
        P("row", "col"),
        P(),
        P(),
        P(),
        P(None, "col"),
        P(None, "row"),
    )
    out_specs = P("row", "col")
    return jax.shard_map(body, mesh=mesh, in_specs=in_specs, out_specs=out_specs, check_vma=False)
```

profile of v0, /device:TPU:1, one launch (start us, length us, event | category | flops | bytes accessed | tf_op | source)
XLA Modules:
  0.0 227.8 jit_solution(790989512550864099)
XLA Ops:
  6.5 0.0 copy-start
  6.5 0.7 compare_select_fusion.9
  7.3 2.3 %scatter_custom_fusion = bf16[256,1024]{1,0:T(8,128)(2,1)S(1)} fusion(s32[256]{0:T(256)S(1)} %compare_select_fusion.9, bf16[256,1024]{1,0:T(8,128)(2,1)} %param.8, bf16[]{:T(256)} %constant.62.clone.1), kind=kCustom, calls=%fused_computation.13 | custom fusion | bytes 524800 | tf_op jit(solution)/shard_map/scatter | solution.py:33
  9.6 1.0 all_to_all.8
  10.6 11.5 %all-to-all-start = ((bf16[128,2,1024]{2,1,0:T(2,128)(2,1)}), bf16[128,2,1024]{2,1,0:T(2,128)(2,1)S(1)}, u32[]{:S(2)}, u32[]{:S(2)}) async-start(bf16[128,2,1024]{2,1,0:T(2,128)(2,1)} %all_to_all.8), calls=%async_computation | async-start | bytes 1048576 | tf_op jit(solution)/shard_map/all_to_all | solution.py:12
  22.1 0.0 all-gather.2.cloned.1.call-start
  22.1 0.8 compare_select_fusion.7
  22.9 0.9 compare_select_fusion.3
  23.8 5.9 %gather_fusion.5 = s32[1024]{0:T(1024)S(1)} fusion(s32[100]{0:T(128)} %param.11, s32[1024]{0:T(1024)S(1)} %broadcast_clamp_fusion.4), kind=kCustom, calls=%fused_computation.5 | custom fusion | bytes 12288 | tf_op jit(solution)/shard_map/gather | solution.py:8
  29.7 5.9 %gather_fusion.4 = s32[1024]{0:T(1024)S(1)} fusion(s32[100]{0:T(128)} %param.11, s32[1024]{0:T(1024)S(1)} %broadcast_clamp_fusion.5), kind=kCustom, calls=%fused_computation.4 | custom fusion | bytes 12288 | tf_op jit(solution)/shard_map/gather | solution.py:8
  35.5 0.0 copy-done
  35.5 0.0 copy-start.1
  35.6 16.7 %gather_fusion.3 = s32[4096]{0:T(1024)S(1)} fusion(s32[800]{0:T(1024)S(1)} %copy-done, s32[4096]{0:T(1024)S(1)} %broadcast_clamp_fusion), kind=kCustom, calls=%fused_computation.3 | custom fusion | bytes 49152 | tf_op jit(solution)/shard_map/gather | solution.py:8
  52.3 16.7 %gather_fusion.2 = s32[4096]{0:T(1024)S(1)} fusion(s32[800]{0:T(1024)S(1)} %copy-done, s32[4096]{0:T(1024)S(1)} %broadcast_clamp_fusion.1), kind=kCustom, calls=%fused_computation.2 | custom fusion | bytes 49152 | tf_op jit(solution)/shard_map/gather | solution.py:8
  69.0 0.1 dynamic_slice.3
  69.1 0.0 all-to-all-done
  69.1 0.2 all_to_all.10
  69.3 1.0 compare_select_fusion.2
  70.3 0.0 all-gather.2.cloned.1.call-update
  70.3 0.0 reduce-scatter.2.cloned.1.call-start
  70.3 0.0 copy-done.1
  70.4 8.6 %gather_fusion.1 = s32[2048]{0:T(1024)S(1)} fusion(s32[800]{0:T(1024)S(1)} %copy-done, s32[2048]{0:T(1024)S(1)} %broadcast_clamp_fusion.2), kind=kCustom, calls=%fused_computation.1 | custom fusion | bytes 24576 | tf_op jit(solution)/shard_map/gather | solution.py:8
  79.0 8.6 %gather_fusion = s32[2048]{0:T(1024)S(1)} fusion(s32[800]{0:T(1024)S(1)} %copy-done, s32[2048]{0:T(1024)S(1)} %broadcast_clamp_fusion.3), kind=kCustom, calls=%fused_computation | custom fusion | bytes 24576 | tf_op jit(solution)/shard_map/gather | solution.py:8
  87.6 54.9 %all-gather.2.cloned.1.call-done = bf16[4096,1024]{1,0:T(8,128)(2,1)} async-done(((bf16[256,1024]{1,0:T(8,128)(2,1)}), bf16[4096,1024]{1,0:T(8,128)(2,1)}) %all-gather.2.cloned.1.call-update) | async-done | bytes 8388624 | tf_op jit(solution)/shard_map/all_gather | solution.py:40
  142.5 24.6 %fusion = f32[2048,1024]{1,0:T(8,128)} fusion(bf16[4096,1024]{1,0:T(8,128)(2,1)} %all-gather.2.cloned.1.call-done, bf16[2048,4096]{1,0:T(8,128)(2,1)} %param.10, s32[4096]{0:T(1024)S(1)} %xor.22, s32[2048]{0:T(1024)S(1)} %xor.21), kind=kOutput, calls=%fused_computation.8 | convolution fusion | flops 17196646400 | bytes 33579008 | tf_op jit(solution)/shard_map/dot_general | solution.py:38
  167.1 0.0 reduce-scatter.2.cloned.1.call-update
  167.1 51.8 %reduce-scatter.2.cloned.1.call-done = f32[2048,128]{1,0:T(8,128)} async-done(((f32[2048,1024]{1,0:T(8,128)}), f32[2048,128]{1,0:T(8,128)}) %reduce-scatter.2.cloned.1.call-update) | async-done | bytes 1048592 | tf_op jit(solution)/shard_map/reduce_scatter | solution.py:43
  218.9 2.1 convert_element_type.3
  (10 shorter events, 0.1 us)
Async XLA Ops:
  6.5 29.0 %copy-start = (s32[800]{0:T(1024)S(1)}, s32[800]{0:T(1024)}, u32[]{:S(2)}) copy-start(s32[800]{0:T(1024)} %param.12) | copy-start | bytes 9604
  10.6 58.5 %all-to-all-start = ((bf16[128,2,1024]{2,1,0:T(2,128)(2,1)}), bf16[128,2,1024]{2,1,0:T(2,128)(2,1)S(1)}, u32[]{:S(2)}, u32[]{:S(2)}) async-start(bf16[128,2,1024]{2,1,0:T(2,128)(2,1)} %all_to_all.8), calls=%async_computation | async-start | bytes 1048576 | tf_op jit(solution)/shard_map/all_to_all | solution.py:12
  22.1 120.5 %all-gather.2.cloned.1.call-start = ((), (), s32[]{:S(2)}) async-start(), calls=%async_computation.2 | async-start | bytes 8912896 | tf_op jit(solution)/shard_map/all_gather | solution.py:40
  35.5 34.8 %copy-start.1 = (s32[2,2048]{1,0:T(2,128)S(1)}, s32[2,2048]{1,0:T(2,128)}, u32[]{:S(2)}) copy-start(s32[2,2048]{1,0:T(2,128)} %param.15) | copy-start | bytes 49156
  70.3 148.7 %reduce-scatter.2.cloned.1.call-start = ((), (), s32[]{:S(2)}) async-start(), calls=%async_computation.3 | async-start | bytes 9437184 | tf_op jit(solution)/shard_map/reduce_scatter | solution.py:43
Sparse Core Ops, SparseCore 0:
  70.4 72.0 all-gather.1
  167.2 51.6 reduce-scatter.1
where the time goes:
time: 228 us
  waiting for transfers between devices  107 us (47%)
  local copies, waits for them, and re-layouts  65.8 us (29%)
  matrix products  24.6 us (11%)
  between operations  13.6 us (6%)
  starting transfers between devices  11.6 us (5%)
  other arithmetic  5.5 us (2%)
    gather x6, local copies, waits for them, and re-layouts, pair_irrep(): return jnp.bitwise_xor(labels[orbitals[0]], labels[orbitals[1]])  62.2 us
    all_gather x1, waiting for transfers between devices, body(): lax.all_gather(masked, 'row', axis=0, tiled=True)  54.9 us
    reduce_scatter x1, waiting for transfers between devices, body(): lax.psum_scatter(partial_sum, 'col', scatter_dimension=1, tiled=True)  51.8 us
    dot_general x1, matrix products, body(): jnp.dot(screened, lax.all_gather(masked, 'row', axis=0, tiled=True), pref...  24.6 us
    all_to_all x1, starting transfers between devices, redistribute(): lax.all_to_all(buffer, ('row', 'col'), split_axis=0, concat_axis=0, tiled...  11.5 us
  transfers between devices with their start and end apart: 3, of which 2 were waited for; matrix products, arithmetic and copies ran while one was open for 28% of the time, Pallas kernels for 0%

commit v1 on v0

--- a/solution.py
+++ b/solution.py
@@ -2,6 +2,22 @@
 import jax.numpy as jnp
 from jax import lax
 from jax.sharding import PartitionSpec as P
+
+
+def collect(x, axis, dim):
+    ways, here, lap = (lax.axis_size(axis), lax.axis_index(axis), x.shape[dim])
+    shape = [n * ways if d == dim else n for d, n in enumerate(x.shape)]
+    full = lax.dynamic_update_slice_in_dim(jnp.zeros(shape, x.dtype), x, here * lap, axis=dim)
+    going_up = going_down = x
+    for far in range(1, ways // 2 + 1):
+        going_up = lax.ppermute(going_up, axis, [(d, (d + 1) % ways) for d in range(ways)])
+        full = lax.dynamic_update_slice_in_dim(full, going_up, (here - far) % ways * lap, axis=dim)
+        if 2 * far < ways:
+            going_down = lax.ppermute(going_down, axis, [(d, (d - 1) % ways) for d in range(ways)])
+            full = lax.dynamic_update_slice_in_dim(
+                full, going_down, (here + far) % ways * lap, axis=dim
+            )
+    return full
 
 
 def pair_irrep(labels, orbitals):
@@ -35,11 +51,7 @@
     own_sym = lax.dynamic_slice_in_dim(k_sym, my_row * stored, stored)
     masked = jnp.where(own_sym[:, None] == occ_sym[None, :], grid_rows, naught)
     screened = jnp.where(m_sym[:, None] == k_sym[None, :], integrals, naught)
-    partial_sum = jnp.dot(
-        screened,
-        lax.all_gather(masked, "row", axis=0, tiled=True),
-        preferred_element_type=jnp.float32,
-    )
+    partial_sum = jnp.dot(screened, collect(masked, "row", 0), preferred_element_type=jnp.float32)
     return lax.psum_scatter(partial_sum, "col", scatter_dimension=1, tiled=True).astype(
         jnp.bfloat16
     )

time: 228 us -> 290 us (1.27)
  starting transfers between devices: 11.6 us -> 45.3 us
  local copies, waits for them, and re-layouts: 65.8 us -> 89.3 us
  waiting for transfers between devices: 107 us -> 110 us
    all_gather x1 -> x0, waiting for transfers between devices: 54.9 us -> none  [body(): lax.all_gather(masked, 'row', axis=0, tiled=True)]
    ppermute x0 -> x15, waiting for transfers between devices: none -> 51.3 us  [the longest x8 50.6 us: collect(): lax.ppermute(going_up, axis, [(d, (d + 1) % ways) for d in range(ways)])]
    ppermute x0 -> x15, starting transfers between devices: none -> 33.8 us  [the longest x7 32.4 us: collect(): lax.ppermute(going_down, axis, [(d, (d - 1) % ways) for d in range(ways)])]
    dynamic_update_slice x0 -> x15, local copies, waits for them, and re-layouts: none -> 17.8 us  [the longest x8 9.84 us: collect(): lax.dynamic_update_slice_in_dim(full, going_up, (here - far) % ways * lap...]
    reduce_scatter x1, waiting for transfers between devices: 51.8 us -> 59.1 us  [body(): lax.psum_scatter(partial_sum, 'col', scatter_dimension=1, tiled=True)]
    broadcast_in_dim x0 -> x1, local copies, waits for them, and re-layouts: none -> 4.29 us  [collect(): jnp.zeros(shape, x.dtype)]
  transfers between devices with their start and end apart: 3 -> 17, of which waited for: 2 -> 9; matrix products, arithmetic and copies ran while one was open for 28% -> 28% of each run, Pallas kernels for 0% -> 0%
where the time goes in v1:
time: 290 us; the launch traced here: 289 us
  waiting for transfers between devices  110 us (38%)
  local copies, waits for them, and re-layouts  89.3 us (31%)
  starting transfers between devices  45.3 us (16%)
  matrix products  24.6 us (8%)
  between operations  13.9 us (5%)
  other arithmetic  5.57 us (2%)
    gather x6, local copies, waits for them, and re-layouts, pair_irrep(): return jnp.bitwise_xor(labels[orbitals[0]], labels[orbitals[1]])  63.7 us
    reduce_scatter x1, waiting for transfers between devices, body(): lax.psum_scatter(partial_sum, 'col', scatter_dimension=1, tiled=True)  59.1 us
    ppermute x8, waiting for transfers between devices, collect(): lax.ppermute(going_up, axis, [(d, (d + 1) % ways) for d in range(ways)])  50.6 us
    ppermute x7, starting transfers between devices, collect(): lax.ppermute(going_down, axis, [(d, (d - 1) % ways) for d in range(ways)])  32.4 us
    dot_general x1, matrix products, body(): jnp.dot(screened, collect(masked, 'row', 0), preferred_element_type=jnp.f...  24.6 us
    all_to_all x1, starting transfers between devices, redistribute(): lax.all_to_all(buffer, ('row', 'col'), split_axis=0, concat_axis=0, tiled...  11.5 us
    dynamic_update_slice x8, local copies, waits for them, and re-layouts, collect(): lax.dynamic_update_slice_in_dim(full, going_up, (here - far) % ways * lap...  9.84 us
    dynamic_update_slice x7, local copies, waits for them, and re-layouts, collect(): lax.dynamic_update_slice_in_dim(full, going_down, (here + far) % ways * l...  7.93 us
  transfers between devices with their start and end apart: 17, of which 9 were waited for; matrix products, arithmetic and copies ran while one was open for 28% of the time, Pallas kernels for 0%

profile of v1, /device:TPU:1, one launch (start us, length us, event | category | flops | bytes accessed | tf_op | source)
XLA Modules:
  0.0 289.1 jit_solution(3996225728944095405)
XLA Ops:
  7.3 2.3 scatter_custom_fusion
  10.6 11.5 %all-to-all-start = ((bf16[128,2,1024]{2,1,0:T(2,128)(2,1)}), bf16[128,2,1024]{2,1,0:T(2,128)(2,1)S(1)}, u32[]{:S(2)}, u32[]{:S(2)}) async-start(bf16[128,2,1024]{2,1,0:T(2,128)(2,1)} %all_to_all.8), calls=%async_computation | async-start | bytes 1048576 | tf_op jit(solution)/shard_map/all_to_all | solution.py:28
  23.8 16.7 %gather_fusion.2 = s32[4096]{0:T(1024)S(1)} fusion(s32[800]{0:T(1024)S(1)} %copy-done, s32[4096]{0:T(1024)S(1)} %broadcast_clamp_fusion.1), kind=kCustom, calls=%fused_computation.2 | custom fusion | bytes 49152 | tf_op jit(solution)/shard_map/gather | solution.py:24
  40.5 16.7 %gather_fusion.3 = s32[4096]{0:T(1024)S(1)} fusion(s32[800]{0:T(1024)S(1)} %copy-done, s32[4096]{0:T(1024)S(1)} %broadcast_clamp_fusion), kind=kCustom, calls=%fused_computation.3 | custom fusion | bytes 49152 | tf_op jit(solution)/shard_map/gather | solution.py:24
  57.2 6.6 %gather_fusion.4 = s32[1024]{0:T(1024)S(1)} fusion(s32[100]{0:T(128)S(1)} %copy-done.1, s32[1024]{0:T(1024)S(1)} %broadcast_clamp_fusion.5), kind=kCustom, calls=%fused_computation.4 | custom fusion | bytes 12288 | tf_op jit(solution)/shard_map/gather | solution.py:24
  63.8 6.6 %gather_fusion.5 = s32[1024]{0:T(1024)S(1)} fusion(s32[100]{0:T(128)S(1)} %copy-done.1, s32[1024]{0:T(1024)S(1)} %broadcast_clamp_fusion.4), kind=kCustom, calls=%fused_computation.5 | custom fusion | bytes 12288 | tf_op jit(solution)/shard_map/gather | solution.py:24
  70.7 4.3 %broadcast_in_dim.11 = bf16[4096,1024]{1,0:T(8,128)(2,1)} broadcast(bf16[]{:T(256)} %constant.143.clone.1), dimensions={} | broadcast | bytes 8388610 | tf_op jit(solution)/shard_map/broadcast_in_dim | solution.py:10
  75.0 1.1 constant_dynamic-update-slice_fusion.15
  76.1 1.3 collective-permute-start
  77.4 3.5 %collective-permute-start.1 = (bf16[256,1024]{1,0:T(8,128)(2,1)S(1)}, bf16[256,1024]{1,0:T(8,128)(2,1)S(1)}, u32[]{:S(2)}, u32[]{:S(2)}) collective-permute-start(bf16[256,1024]{1,0:T(8,128)(2,1)S(1)} %get-tuple-element.6), channel_id=1, source_target_pairs={{0,120},{8,0},{16,8},{24,16},{32,24},{40,32},{48,40},{56,48},{64,5... | collective-permute-start | bytes 1572872 | tf_op jit(solution)/shard_map/ppermute | solution.py:16
  80.9 10.9 %collective-permute-done = bf16[256,1024]{1,0:T(8,128)(2,1)S(1)} collective-permute-done((bf16[256,1024]{1,0:T(8,128)(2,1)S(1)}, bf16[256,1024]{1,0:T(8,128)(2,1)S(1)}, u32[]{:S(2)}, u32[]{:S(2)}) %collective-permute-start) | collective-permute-done | bytes 524320 | tf_op jit(solution)/shard_map/ppermute | solution.py:13
  91.7 4.8 %collective-permute-start.3 = (bf16[256,1024]{1,0:T(8,128)(2,1)S(1)}, bf16[256,1024]{1,0:T(8,128)(2,1)S(1)}, u32[]{:S(2)}, u32[]{:S(2)}) collective-permute-start(bf16[256,1024]{1,0:T(8,128)(2,1)S(1)} %collective-permute-done.1), channel_id=1, source_target_pairs={{0,120},{8,0},{16,8},{24,16},{32,24},{40,32},{48,40},{56,48},{64,5... | collective-permute-start | bytes 1572872 | tf_op jit(solution)/shard_map/ppermute | solution.py:16
  96.5 10.0 %collective-permute-done.2 = bf16[256,1024]{1,0:T(8,128)(2,1)S(1)} collective-permute-done((bf16[256,1024]{1,0:T(8,128)(2,1)S(1)}, bf16[256,1024]{1,0:T(8,128)(2,1)S(1)}, u32[]{:S(2)}, u32[]{:S(2)}) %collective-permute-start.2) | collective-permute-done | bytes 524320 | tf_op jit(solution)/shard_map/ppermute | solution.py:13
  106.5 4.8 %collective-permute-start.5 = (bf16[256,1024]{1,0:T(8,128)(2,1)S(1)}, bf16[256,1024]{1,0:T(8,128)(2,1)S(1)}, u32[]{:S(2)}, u32[]{:S(2)}) collective-permute-start(bf16[256,1024]{1,0:T(8,128)(2,1)S(1)} %collective-permute-done.3), channel_id=1, source_target_pairs={{0,120},{8,0},{16,8},{24,16},{32,24},{40,32},{48,40},{56,48},{64,5... | collective-permute-start | bytes 1572872 | tf_op jit(solution)/shard_map/ppermute | solution.py:16
  111.3 9.0 %collective-permute-done.4 = bf16[256,1024]{1,0:T(8,128)(2,1)S(1)} collective-permute-done((bf16[256,1024]{1,0:T(8,128)(2,1)S(1)}, bf16[256,1024]{1,0:T(8,128)(2,1)S(1)}, u32[]{:S(2)}, u32[]{:S(2)}) %collective-permute-start.4) | collective-permute-done | bytes 524320 | tf_op jit(solution)/shard_map/ppermute | solution.py:13
  120.3 4.8 %collective-permute-start.7 = (bf16[256,1024]{1,0:T(8,128)(2,1)S(1)}, bf16[256,1024]{1,0:T(8,128)(2,1)}, u32[]{:S(2)}, u32[]{:S(2)}) collective-permute-start(bf16[256,1024]{1,0:T(8,128)(2,1)S(1)} %collective-permute-done.5), channel_id=1, source_target_pairs={{0,120},{8,0},{16,8},{24,16},{32,24},{40,32},{48,40},{56,48},{64,5... | collective-permute-start | bytes 1572872 | tf_op jit(solution)/shard_map/ppermute | solution.py:16
  125.1 8.1 %collective-permute-done.6 = bf16[256,1024]{1,0:T(8,128)(2,1)S(1)} collective-permute-done((bf16[256,1024]{1,0:T(8,128)(2,1)S(1)}, bf16[256,1024]{1,0:T(8,128)(2,1)S(1)}, u32[]{:S(2)}, u32[]{:S(2)}) %collective-permute-start.6) | collective-permute-done | bytes 524320 | tf_op jit(solution)/shard_map/ppermute | solution.py:13
  133.3 4.8 %collective-permute-start.9 = (bf16[256,1024]{1,0:T(8,128)(2,1)}, bf16[256,1024]{1,0:T(8,128)(2,1)}, u32[]{:S(2)}, u32[]{:S(2)}) collective-permute-start(bf16[256,1024]{1,0:T(8,128)(2,1)} %collective-permute-done.7), channel_id=1, source_target_pairs={{0,120},{8,0},{16,8},{24,16},{32,24},{40,32},{48,40},{56,48},{64,5... | collective-permute-start | bytes 1572872 | tf_op jit(solution)/shard_map/ppermute | solution.py:16
  138.1 7.1 %collective-permute-done.8 = bf16[256,1024]{1,0:T(8,128)(2,1)S(1)} collective-permute-done((bf16[256,1024]{1,0:T(8,128)(2,1)S(1)}, bf16[256,1024]{1,0:T(8,128)(2,1)S(1)}, u32[]{:S(2)}, u32[]{:S(2)}) %collective-permute-start.8) | collective-permute-done | bytes 524320 | tf_op jit(solution)/shard_map/ppermute | solution.py:13
  145.5 8.6 %gather_fusion = s32[2048]{0:T(1024)S(1)} fusion(s32[800]{0:T(1024)S(1)} %copy-done, s32[2048]{0:T(1024)S(1)} %broadcast_clamp_fusion.3), kind=kCustom, calls=%fused_computation | custom fusion | bytes 24576 | tf_op jit(solution)/shard_map/gather | solution.py:24
  154.0 8.6 %gather_fusion.1 = s32[2048]{0:T(1024)S(1)} fusion(s32[800]{0:T(1024)S(1)} %copy-done, s32[2048]{0:T(1024)S(1)} %broadcast_clamp_fusion.2), kind=kCustom, calls=%fused_computation.1 | custom fusion | bytes 24576 | tf_op jit(solution)/shard_map/gather | solution.py:24
  164.4 1.9 constant_dynamic-update-slice_fusion.12
  166.3 4.6 %collective-permute-start.11 = (bf16[256,1024]{1,0:T(8,128)(2,1)}, bf16[256,1024]{1,0:T(8,128)(2,1)S(1)}, u32[]{:S(2)}, u32[]{:S(2)}) collective-permute-start(bf16[256,1024]{1,0:T(8,128)(2,1)} %collective-permute-done.9), channel_id=1, source_target_pairs={{0,120},{8,0},{16,8},{24,16},{32,24},{40,32},{48,40},{56,48},{64,5... | collective-permute-start | bytes 1572872 | tf_op jit(solution)/shard_map/ppermute | solution.py:16
  173.4 1.9 constant_dynamic-update-slice_fusion.8
  175.3 1.9 constant_dynamic-update-slice_fusion.7
  177.3 5.1 %collective-permute-start.13 = (bf16[256,1024]{1,0:T(8,128)(2,1)S(1)}, bf16[256,1024]{1,0:T(8,128)(2,1)S(1)}, u32[]{:S(2)}, u32[]{:S(2)}) collective-permute-start(bf16[256,1024]{1,0:T(8,128)(2,1)S(1)} %collective-permute-done.11), channel_id=1, source_target_pairs={{0,120},{8,0},{16,8},{24,16},{32,24},{40,32},{48,40},{56,48},{64,5... | collective-permute-start | bytes 1572872 | tf_op jit(solution)/shard_map/ppermute | solution.py:16
  183.3 1.9 constant_dynamic-update-slice_fusion.5
  185.2 1.9 constant_dynamic-update-slice_fusion.4
  190.1 5.5 %collective-permute-done.14 = bf16[256,1024]{1,0:T(8,128)(2,1)S(1)} collective-permute-done((bf16[256,1024]{1,0:T(8,128)(2,1)S(1)}, bf16[256,1024]{1,0:T(8,128)(2,1)S(1)}, u32[]{:S(2)}, u32[]{:S(2)}) %collective-permute-start.14) | collective-permute-done | bytes 524320 | tf_op jit(solution)/shard_map/ppermute | solution.py:13
  196.5 24.6 %fusion = f32[2048,1024]{1,0:T(8,128)} fusion(bf16[4096,1024]{1,0:T(8,128)(2,1)} %constant_dynamic-update-slice_fusion, bf16[2048,4096]{1,0:T(8,128)(2,1)} %param.10, s32[4096]{0:T(1024)S(1)} %xor.22, s32[2048]{0:T(1024)S(1)} %xor.21), kind=kOutput, calls=%fused_computation.8 | convolution fusion | flops 17196646400 | bytes 33579008 | tf_op jit(solution)/shard_map/dot_general | solution.py:54
  221.1 59.1 %reduce-scatter.2.cloned.1.call-done = f32[2048,128]{1,0:T(8,128)} async-done(((f32[2048,1024]{1,0:T(8,128)}), f32[2048,128]{1,0:T(8,128)}) %reduce-scatter.2.cloned.1.call-update) | async-done | bytes 1048592 | tf_op jit(solution)/shard_map/reduce_scatter | solution.py:55
  280.2 2.1 convert_element_type.3
  (55 shorter events, 13.0 us)
Async XLA Ops:
  6.5 17.3 %copy-start = (s32[800]{0:T(1024)S(1)}, s32[800]{0:T(1024)}, u32[]{:S(2)}) copy-start(s32[800]{0:T(1024)} %param.12) | copy-start | bytes 9604
  10.6 60.0 %all-to-all-start = ((bf16[128,2,1024]{2,1,0:T(2,128)(2,1)}), bf16[128,2,1024]{2,1,0:T(2,128)(2,1)S(1)}, u32[]{:S(2)}, u32[]{:S(2)}) async-start(bf16[128,2,1024]{2,1,0:T(2,128)(2,1)} %all_to_all.8), calls=%async_computation | async-start | bytes 1048576 | tf_op jit(solution)/shard_map/all_to_all | solution.py:28
  22.1 258.1 %reduce-scatter.2.cloned.1.call-start = ((), (), s32[]{:S(2)}) async-start(), calls=%async_computation.2 | async-start | bytes 9437184 | tf_op jit(solution)/shard_map/reduce_scatter | solution.py:55
  40.5 16.7 %copy-start.1 = (s32[100]{0:T(128)S(1)}, s32[100]{0:T(128)}, u32[]{:S(2)}) copy-start(s32[100]{0:T(128)} %param.11) | copy-start | bytes 1204
  63.8 69.4 %copy-start.4 = (s32[2,2048]{1,0:T(2,128)S(1)}, s32[2,2048]{1,0:T(2,128)}, u32[]{:S(2)}) copy-start(s32[2,2048]{1,0:T(2,128)} %param.15) | copy-start | bytes 49156
  76.1 15.7 %collective-permute-start = (bf16[256,1024]{1,0:T(8,128)(2,1)S(1)}, bf16[256,1024]{1,0:T(8,128)(2,1)S(1)}, u32[]{:S(2)}, u32[]{:S(2)}) collective-permute-start(bf16[256,1024]{1,0:T(8,128)(2,1)S(1)} %get-tuple-element.6), channel_id=1, source_target_pairs={{0,8},{8,16},{16,24},{24,32},{32,40},{40,48},{48,56},{56,64},{64,7... | collective-permute-start | bytes 1572872 | tf_op jit(solution)/shard_map/ppermute | solution.py:13
  77.4 14.4 %collective-permute-start.1 = (bf16[256,1024]{1,0:T(8,128)(2,1)S(1)}, bf16[256,1024]{1,0:T(8,128)(2,1)S(1)}, u32[]{:S(2)}, u32[]{:S(2)}) collective-permute-start(bf16[256,1024]{1,0:T(8,128)(2,1)S(1)} %get-tuple-element.6), channel_id=1, source_target_pairs={{0,120},{8,0},{16,8},{24,16},{32,24},{40,32},{48,40},{56,48},{64,5... | collective-permute-start | bytes 1572872 | tf_op jit(solution)/shard_map/ppermute | solution.py:16
  91.7 14.7 %collective-permute-start.2 = (bf16[256,1024]{1,0:T(8,128)(2,1)S(1)}, bf16[256,1024]{1,0:T(8,128)(2,1)S(1)}, u32[]{:S(2)}, u32[]{:S(2)}) collective-permute-start(bf16[256,1024]{1,0:T(8,128)(2,1)S(1)} %collective-permute-done), channel_id=1, source_target_pairs={{0,8},{8,16},{16,24},{24,32},{32,40},{40,48},{48,56},{56,64},{64,7... | collective-permute-start | bytes 1572872 | tf_op jit(solution)/shard_map/ppermute | solution.py:13
  91.7 14.7 %collective-permute-start.3 = (bf16[256,1024]{1,0:T(8,128)(2,1)S(1)}, bf16[256,1024]{1,0:T(8,128)(2,1)S(1)}, u32[]{:S(2)}, u32[]{:S(2)}) collective-permute-start(bf16[256,1024]{1,0:T(8,128)(2,1)S(1)} %collective-permute-done.1), channel_id=1, source_target_pairs={{0,120},{8,0},{16,8},{24,16},{32,24},{40,32},{48,40},{56,48},{64,5... | collective-permute-start | bytes 1572872 | tf_op jit(solution)/shard_map/ppermute | solution.py:16
  106.5 18.6 %copy-start.3 = (bf16[256,1024]{1,0:T(8,128)(2,1)}, bf16[256,1024]{1,0:T(8,128)(2,1)S(1)}, u32[]{:S(2)}) copy-start(bf16[256,1024]{1,0:T(8,128)(2,1)S(1)} %collective-permute-done.2) | copy-start | bytes 1572868
  106.5 13.8 %collective-permute-start.4 = (bf16[256,1024]{1,0:T(8,128)(2,1)S(1)}, bf16[256,1024]{1,0:T(8,128)(2,1)S(1)}, u32[]{:S(2)}, u32[]{:S(2)}) collective-permute-start(bf16[256,1024]{1,0:T(8,128)(2,1)S(1)} %collective-permute-done.2), channel_id=1, source_target_pairs={{0,8},{8,16},{16,24},{24,32},{32,40},{40,48},{48,56},{56,64},{64,7... | collective-permute-start | bytes 1572872 | tf_op jit(solution)/shard_map/ppermute | solution.py:13
  106.5 13.8 %collective-permute-start.5 = (bf16[256,1024]{1,0:T(8,128)(2,1)S(1)}, bf16[256,1024]{1,0:T(8,128)(2,1)S(1)}, u32[]{:S(2)}, u32[]{:S(2)}) collective-permute-start(bf16[256,1024]{1,0:T(8,128)(2,1)S(1)} %collective-permute-done.3), channel_id=1, source_target_pairs={{0,120},{8,0},{16,8},{24,16},{32,24},{40,32},{48,40},{56,48},{64,5... | collective-permute-start | bytes 1572872 | tf_op jit(solution)/shard_map/ppermute | solution.py:16
  120.3 12.9 %collective-permute-start.6 = (bf16[256,1024]{1,0:T(8,128)(2,1)S(1)}, bf16[256,1024]{1,0:T(8,128)(2,1)S(1)}, u32[]{:S(2)}, u32[]{:S(2)}) collective-permute-start(bf16[256,1024]{1,0:T(8,128)(2,1)S(1)} %collective-permute-done.4), channel_id=1, source_target_pairs={{0,8},{8,16},{16,24},{24,32},{32,40},{40,48},{48,56},{56,64},{64,7... | collective-permute-start | bytes 1572872 | tf_op jit(solution)/shard_map/ppermute | solution.py:13
  120.3 13.0 %collective-permute-start.7 = (bf16[256,1024]{1,0:T(8,128)(2,1)S(1)}, bf16[256,1024]{1,0:T(8,128)(2,1)}, u32[]{:S(2)}, u32[]{:S(2)}) collective-permute-start(bf16[256,1024]{1,0:T(8,128)(2,1)S(1)} %collective-permute-done.5), channel_id=1, source_target_pairs={{0,120},{8,0},{16,8},{24,16},{32,24},{40,32},{48,40},{56,48},{64,5... | collective-permute-start | bytes 1572872 | tf_op jit(solution)/shard_map/ppermute | solution.py:16
  133.2 12.0 %copy-start.2 = (bf16[256,1024]{1,0:T(8,128)(2,1)}, bf16[256,1024]{1,0:T(8,128)(2,1)S(1)}, u32[]{:S(2)}) copy-start(bf16[256,1024]{1,0:T(8,128)(2,1)S(1)} %collective-permute-done.6) | copy-start | bytes 1572868
  133.2 12.0 %collective-permute-start.8 = (bf16[256,1024]{1,0:T(8,128)(2,1)S(1)}, bf16[256,1024]{1,0:T(8,128)(2,1)S(1)}, u32[]{:S(2)}, u32[]{:S(2)}) collective-permute-start(bf16[256,1024]{1,0:T(8,128)(2,1)S(1)} %collective-permute-done.6), channel_id=1, source_target_pairs={{0,8},{8,16},{16,24},{24,32},{32,40},{40,48},{48,56},{56,64},{64,7... | collective-permute-start | bytes 1572872 | tf_op jit(solution)/shard_map/ppermute | solution.py:13
  133.3 33.0 %collective-permute-start.9 = (bf16[256,1024]{1,0:T(8,128)(2,1)}, bf16[256,1024]{1,0:T(8,128)(2,1)}, u32[]{:S(2)}, u32[]{:S(2)}) collective-permute-start(bf16[256,1024]{1,0:T(8,128)(2,1)} %collective-permute-done.7), channel_id=1, source_target_pairs={{0,120},{8,0},{16,8},{24,16},{32,24},{40,32},{48,40},{56,48},{64,5... | collective-permute-start | bytes 1572872 | tf_op jit(solution)/shard_map/ppermute | solution.py:16
  145.2 26.5 %collective-permute-start.10 = (bf16[256,1024]{1,0:T(8,128)(2,1)S(1)}, bf16[256,1024]{1,0:T(8,128)(2,1)}, u32[]{:S(2)}, u32[]{:S(2)}) collective-permute-start(bf16[256,1024]{1,0:T(8,128)(2,1)S(1)} %collective-permute-done.8), channel_id=1, source_target_pairs={{0,8},{8,16},{16,24},{24,32},{32,40},{40,48},{48,56},{56,64},{64,7... | collective-permute-start | bytes 1572872 | tf_op jit(solution)/shard_map/ppermute | solution.py:13
  166.3 11.1 %collective-permute-start.11 = (bf16[256,1024]{1,0:T(8,128)(2,1)}, bf16[256,1024]{1,0:T(8,128)(2,1)S(1)}, u32[]{:S(2)}, u32[]{:S(2)}) collective-permute-start(bf16[256,1024]{1,0:T(8,128)(2,1)} %collective-permute-done.9), channel_id=1, source_target_pairs={{0,120},{8,0},{16,8},{24,16},{32,24},{40,32},{48,40},{56,48},{64,5... | collective-permute-start | bytes 1572872 | tf_op jit(solution)/shard_map/ppermute | solution.py:16
  171.7 11.6 %collective-permute-start.12 = (bf16[256,1024]{1,0:T(8,128)(2,1)}, bf16[256,1024]{1,0:T(8,128)(2,1)S(1)}, u32[]{:S(2)}, u32[]{:S(2)}) collective-permute-start(bf16[256,1024]{1,0:T(8,128)(2,1)} %collective-permute-done.10), channel_id=1, source_target_pairs={{0,8},{8,16},{16,24},{24,32},{32,40},{40,48},{48,56},{56,64},{64,7... | collective-permute-start | bytes 1572872 | tf_op jit(solution)/shard_map/ppermute | solution.py:13
  177.3 11.9 %collective-permute-start.13 = (bf16[256,1024]{1,0:T(8,128)(2,1)S(1)}, bf16[256,1024]{1,0:T(8,128)(2,1)S(1)}, u32[]{:S(2)}, u32[]{:S(2)}) collective-permute-start(bf16[256,1024]{1,0:T(8,128)(2,1)S(1)} %collective-permute-done.11), channel_id=1, source_target_pairs={{0,120},{8,0},{16,8},{24,16},{32,24},{40,32},{48,40},{56,48},{64,5... | collective-permute-start | bytes 1572872 | tf_op jit(solution)/shard_map/ppermute | solution.py:16
  183.3 12.3 %collective-permute-start.14 = (bf16[256,1024]{1,0:T(8,128)(2,1)S(1)}, bf16[256,1024]{1,0:T(8,128)(2,1)S(1)}, u32[]{:S(2)}, u32[]{:S(2)}) collective-permute-start(bf16[256,1024]{1,0:T(8,128)(2,1)S(1)} %collective-permute-done.12), channel_id=1, source_target_pairs={{0,8},{8,16},{16,24},{24,32},{32,40},{40,48},{48,56},{56,64},{64,7... | collective-permute-start | bytes 1572872 | tf_op jit(solution)/shard_map/ppermute | solution.py:13
Sparse Core Ops, SparseCore 0:
  221.2 58.9 reduce-scatter.1
